TPU v7x, 256 devices: a whole 4x4x8 slice. The times are simulated.
256 devices in a mesh: row: 8 (over z_hi, core), col: 32 (over x, z_lo, y).
Axes of the slice: x: 4, y: 4, z: 8 (z_hi: 4, z_lo: 2; z = z_hi * 2 + z_lo), core: 2. Of those that a mesh axis runs over, the one named last changes fastest.
Arguments:
- grad_out: bfloat16 [98304, 512], P(('row', 'col')), may hold values from -6 to 6
- features: bfloat16 [98304, 512], P(('row', 'col')), may hold values from -0.01953125 to 0.01953125
- weight: bfloat16 [512, 512], replicated, may hold values from -0.25 to 0.25
- degrees: int32 [98304], P(('row', 'col')), may hold values from 1 to 16
- block_coords: int32 [8, 32, 160, 2], P('row', 'col'), may hold values from 0 to 95, as said below
- block_values: bfloat16 [8, 32, 160, 128, 128], P('row', 'col'), may hold values from -0.21875 to 0.21875
- block_counts: int32 [8, 32], P('row', 'col'), may hold values from 1 to 160, as said below
Outputs:
- grad_features: bfloat16 [98304, 512], P(('row', 'col'))
- grad_weight: float32 [512, 512], replicated
Inputs may be any that keep to these rules, and one draw needn't show every extreme that they name: `block_counts`: each tile has 1 to 160 live slots, and some tile has exactly 160. `block_coords`: within a tile the 160 slots name distinct blocks; the first coordinate is below 24, the second below 96.
All inputs are finite; a program needn't handle non-finite values.
Results may differ from a plain program's by a relative error of at most 0.02.
Values may be sent and summed in bfloat16 or wider, within the bound.
A program may use at most 192 MiB of HBM per device.

v0:
```python
import jax
import jax.numpy as jnp
from jax import lax
from jax.sharding import PartitionSpec as P


def body(grad_out, features, weight, degrees, block_coords, block_values, block_counts):
    block_edge = block_values.shape[-1]
    feat_width = grad_out.shape[1]
    inv_root = lax.rsqrt(degrees.astype(jnp.float32))
    scaled = (grad_out.astype(jnp.float32) * inv_root[:, None]).astype(jnp.bfloat16)
    gathered = lax.all_gather(scaled, "row", axis=0, tiled=True)
    source = gathered.reshape(gathered.shape[0] // block_edge, block_edge, feat_width)
    tile_coords = block_coords[0, 0]
    tile_values = block_values[0, 0]
    live_count = block_counts[0, 0]
    slot_group = 32
    out_blocks = lax.axis_size("col") * grad_out.shape[0] // block_edge

    def accumulate(step_index, partial_acc):
        slot_start = step_index * slot_group
        slot_pair = lax.dynamic_slice_in_dim(tile_coords, slot_start, slot_group, 0)
        slot_blocks = lax.dynamic_slice_in_dim(tile_values, slot_start, slot_group, 0)
        picked = source[slot_pair[:, 0], :, 0 : 0 + feat_width]
        slot_live = slot_start + jnp.arange(slot_group, dtype=jnp.int32) < live_count
        contribution = jnp.einsum(
            "sab,saf->sbf", slot_blocks, picked, preferred_element_type=jnp.float32
        )
        contribution = jnp.where(slot_live[:, None, None], contribution, jnp.float32(0.0))
        return partial_acc.at[slot_pair[:, 1]].add(contribution)

    trip_count = (live_count + slot_group - 1) // slot_group
    initial = jnp.zeros((out_blocks, block_edge, feat_width), jnp.float32)
    finished = lax.fori_loop(0, trip_count, accumulate, initial)
    aggregated = lax.psum_scatter(
        finished.reshape(out_blocks * block_edge, feat_width).astype(jnp.bfloat16),
        "col",
        scatter_dimension=0,
        tiled=True,
    ).astype(jnp.float32)
    grad_agg = (aggregated * inv_root[:, None]).astype(jnp.bfloat16)
    grad_features = lax.dot_general(
        grad_agg, weight, (((1,), (1,)), ((), ())), preferred_element_type=jnp.float32
    ).astype(jnp.bfloat16)
    local_weight = lax.dot_general(
        features, grad_agg, (((0,), (0,)), ((), ())), preferred_element_type=jnp.float32
    )
    grad_weight = lax.psum(local_weight, ("row", "col"))
    return (grad_features, grad_weight)


def solution(mesh):
    in_specs = (
        P(("row", "col"), None),
        P(("row", "col"), None),
        P(),
        P(("row", "col")),
        P("row", "col", None, None),
        P("row", "col", None, None, None),
        P("row", "col"),
    )
    out_specs = (P(("row", "col"), None), P())
    return jax.shard_map(body, mesh=mesh, in_specs=in_specs, out_specs=out_specs, check_vma=False)
```

profile of v0, /device:TPU:1, one launch (start us, length us, event | category | flops | bytes accessed | tf_op | source)
XLA Modules:
  0.0 696.3 jit_solution(13707821826210191376)
XLA Ops:
  7.2 0.0 copy-start
  7.2 0.0 all-gather.2.cloned.1.call-start
  7.2 0.7 convert_rsqrt_fusion
  8.0 1.9 multiply_convert_fusion.1
  9.8 0.0 all-gather.2.cloned.1.call-update
  9.9 0.0 reduce-scatter.2.cloned.1.call-start
  10.6 8.1 %copy.9 = bf16[1,1,160,128,128]{3,4,2,1,0:T(8,128)(2,1)} copy(bf16[1,1,160,128,128]{4,3,2,1,0:T(8,128)(2,1)} %param.14) | data formatting | bytes 10485760 | tf_op args[5]
  18.7 40.3 %all-gather.2.cloned.1.call-done = bf16[3072,512]{1,0:T(8,128)(2,1)} async-done(((bf16[384,512]{1,0:T(8,128)(2,1)}), bf16[3072,512]{1,0:T(8,128)(2,1)}) %all-gather.2.cloned.1.call-update) | async-done | bytes 3145744 | tf_op jit(solution)/shard_map/all_gather | solution.py:12
  59.0 11.5 %broadcast_in_dim.20 = f32[96,128,512]{2,1,0:T(8,128)} broadcast(f32[]{:T(128)} %constant.32.clone.1), dimensions={} | broadcast | bytes 25165828 | tf_op jit(solution)/shard_map/broadcast_in_dim | solution.py:33
  70.6 0.0 copy-done.2
  70.6 62.5 %while.10 = (s32[]{:T(128)}, f32[96,128,512]{2,1,0:T(8,128)}, s32[]{:T(128)}, s32[160,2]{0,1:T(2,128)S(1)}, s32[]{:T(128)}, /*index=5*/bf16[160,128,128]{1,2,0:T...) while((s32[]{:T(128)}, f32[96,128,512]{2,1,0:T(8,128)}, ...), condition=%wide.region_2.3_spmd, body=%wide.region_0.2_spmd.sunk | while | flops 541066496 | bytes 47191656 | solution.py:34
  70.6 0.7 add_compare_fusion.2
  71.2 0.1 constant_dynamic-slice_fusion.2
  71.3 4.7 gather_fusion
  76.0 7.0 %broadcast_select_fusion.2 = f32[32,128,512]{2,1,0:T(8,128)} fusion(pred[32]{0:T(512)(128)(4,1)S(1)} %add_compare_fusion.2, bf16[32,128,512]{2,1,0:T(8,128)(2,1)} %gather_fusion, bf16[160,128,128]{1,2,0:T(8,128)(2,1)} %get-tuple-element.134, s32[]{:T(128)S(6)} %select_n.34), kind=kOutput, calls=%fused_computation.2.clone.1 | convolution fusion | flops 538968064 | bytes 13631524 | tf_op jit(solution)/shard_map/while/body/sab,saf->sbf/dot_general | solution.py:26
  83.0 18.8 %scatter_fusion = f32[96,128,512]{2,1,0:T(8,128)} fusion(f32[96,128,512]{2,1,0:T(8,128)} %get-tuple-element.119, s32[32]{0:T(128)S(1)} %get-tuple-element.105, f32[32,128,512]{2,1,0:T(8,128)} %broadcast_select_fusion.2), kind=kCustom, calls=%fused_computation.1.clone.1 | custom fusion | flops 2097152 | bytes 25165952 | tf_op jit(solution)/shard_map/while/body/scatter-add | solution.py:30
  101.7 0.7 add_compare_fusion.2
  102.4 0.1 constant_dynamic-slice_fusion.2
  102.5 4.7 gather_fusion
  107.2 7.0 %broadcast_select_fusion.2 = f32[32,128,512]{2,1,0:T(8,128)} fusion(pred[32]{0:T(512)(128)(4,1)S(1)} %add_compare_fusion.2, bf16[32,128,512]{2,1,0:T(8,128)(2,1)} %gather_fusion, bf16[160,128,128]{1,2,0:T(8,128)(2,1)} %get-tuple-element.134, s32[]{:T(128)S(6)} %select_n.34), kind=kOutput, calls=%fused_computation.2.clone.1 | convolution fusion | flops 538968064 | bytes 13631524 | tf_op jit(solution)/shard_map/while/body/sab,saf->sbf/dot_general | solution.py:26
  114.1 18.9 %scatter_fusion = f32[96,128,512]{2,1,0:T(8,128)} fusion(f32[96,128,512]{2,1,0:T(8,128)} %get-tuple-element.119, s32[32]{0:T(128)S(1)} %get-tuple-element.105, f32[32,128,512]{2,1,0:T(8,128)} %broadcast_select_fusion.2), kind=kCustom, calls=%fused_computation.1.clone.1 | custom fusion | flops 2097152 | bytes 25165952 | tf_op jit(solution)/shard_map/while/body/scatter-add | solution.py:30
  133.1 13.3 %convert_element_type.27 = bf16[96,128,512]{2,1,0:T(8,128)(2,1)} convert(f32[96,128,512]{2,1,0:T(8,128)} %get-tuple-element.40) | non-fusion elementwise | flops 6291456 | bytes 37748736 | tf_op jit(solution)/shard_map/convert_element_type | solution.py:36
  146.4 0.0 reduce-scatter.2.cloned.1.call-update
  146.4 0.0 all-reduce.2.cloned.1.call-start
  146.4 262.5 %reduce-scatter.2.cloned.1.call-done = bf16[384,512]{1,0:T(8,128)(2,1)} async-done(((bf16[12288,512]{1,0:T(8,128)(2,1)}), bf16[384,512]{1,0:T(8,128)(2,1)}) %reduce-scatter.2.cloned.1.call-update) | async-done | bytes 393232 | tf_op jit(solution)/shard_map/reduce_scatter | solution.py:35
  408.9 0.0 copy-done.1
  408.9 2.5 convolution_bitcast_fusion
  411.5 0.0 all-reduce.2.cloned.1.call-update
  411.5 0.0 copy-done
  411.5 2.2 convolution_convert_fusion
  413.7 273.5 %all-reduce.2.cloned.1.call-done = f32[512,512]{0,1:T(8,128)} async-done(((f32[512,512]{0,1:T(8,128)}), f32[512,512]{0,1:T(8,128)}) %all-reduce.2.cloned.1.call-update) | async-done | bytes 1048592 | tf_op jit(solution)/shard_map/psum | solution.py:48
  687.2 2.5 copy.10
  (6 shorter events, 0.0 us)
Async XLA Ops:
  7.2 404.3 %copy-start = (bf16[512,512]{1,0:T(8,128)(2,1)S(1)}, bf16[512,512]{1,0:T(8,128)(2,1)}, u32[]{:S(2)}) copy-start(bf16[512,512]{1,0:T(8,128)(2,1)} %param.11) | copy-start | bytes 1572868
  7.2 51.8 %all-gather.2.cloned.1.call-start = ((), (), s32[]{:S(2)}) async-start(), calls=%async_computation.1 | async-start | bytes 3538944 | tf_op jit(solution)/shard_map/all_gather | solution.py:12
  9.9 399.1 %reduce-scatter.2.cloned.1.call-start = ((), (), s32[]{:S(2)}) async-start(), calls=%async_computation.2 | async-start | bytes 12976128 | tf_op jit(solution)/shard_map/reduce_scatter | solution.py:35
  59.0 11.5 %copy-start.2 = (s32[1,1,160,2]{2,3,1,0:T(2,128)S(1)}, s32[1,1,160,2]{2,3,1,0:T(2,128)}, u32[]{:S(2)}) copy-start(s32[1,1,160,2]{2,3,1,0:T(2,128)} %param.13) | copy-start | bytes 3844
  146.4 262.6 %copy-start.1 = (bf16[384,512]{1,0:T(8,128)(2,1)S(1)}, bf16[384,512]{1,0:T(8,128)(2,1)}, u32[]{:S(2)}) copy-start(bf16[384,512]{1,0:T(8,128)(2,1)} %param.10) | copy-start | bytes 1179652
  146.4 540.8 %all-reduce.2.cloned.1.call-start = ((), (), s32[]{:S(2)}) async-start(), calls=%async_computation.3 | async-start | bytes 2097152 | tf_op jit(solution)/shard_map/psum | solution.py:48
Sparse Core Ops, SparseCore 0:
  10.4 48.5 all-gather.1
  146.5 262.3 reduce-scatter.1
  415.0 272.1 all-reduce.1
where the time goes:
time: 698 us; the launch traced here: 696 us
  waiting for transfers between devices  576 us (83%)
  other arithmetic  55 us (8%)
  local copies, waits for them, and re-layouts  31.7 us (5%)
  matrix products  18.6 us (3%)
  between operations  14.4 us (2%)
    psum x1, waiting for transfers between devices, body(): grad_weight = lax.psum(local_weight, ('row', 'col'))  274 us
    reduce_scatter x1, waiting for transfers between devices, body(): lax.psum_scatter(finished.reshape(out_blocks * block_edge, feat_width).as...  263 us
    all_gather x1, waiting for transfers between devices, body(): gathered = lax.all_gather(scaled, 'row', axis=0, tiled=True)  40.3 us
    scatter-add x2, other arithmetic, accumulate(): return partial_acc.at[slot_pair[:, 1]].add(contribution)  37.7 us
  transfers between devices with their start and end apart: 3, of which 3 were waited for; matrix products, arithmetic and copies ran while one was open for 1% of the time, Pallas kernels for 0%

commit v1 on v0

v1 whole, which is shorter than its diff:
```python
import functools

import jax
import jax.numpy as jnp
from jax import lax
from jax.experimental import pallas as pl
from jax.experimental.pallas import tpu as pltpu
from jax.sharding import PartitionSpec as P

MESH = pl.DeviceIdType.MESH
F32, BF16 = jnp.float32, jnp.bfloat16
CAP = 160
EDGE = 128
COLS = 96
PER = 3
PARTS = 4


def fused(
    meta, values_hbm, source_hbm, scale, features, weight,
    out_features, out_weight,
    values, source, run, part, ring1, ring2, mid, ring3, ring4, last_sum, z_in, agg,
    w_send, w_own, w_in, w_plane, w_piece, w_line, w_z, w_full, w_sib,
    load_sem, ring_send, ring_recv, z_send, z_recv, sib_send, sib_recv,
    plane_send, plane_recv, line_send, line_recv,
):
    row, col = lax.axis_index("row"), lax.axis_index("col")
    core = lax.rem(row, 2)
    z_hi = row // 2
    x, z_lo, y = col // 8, lax.rem(col // 4, 2), lax.rem(col, 4)
    z = z_hi * 2 + z_lo
    plane = x * 4 + y

    def at(ix=x, iz=z, iy=y, icore=core):
        return ((iz // 2) * 2 + icore, (ix * 2 + lax.rem(iz, 2)) * 4 + iy)

    def plane_dev(p):
        return at(ix=p // 4, iy=lax.rem(p, 4))

    sibling = at(icore=1 - core)

    load_v = pltpu.make_async_copy(values_hbm, values, load_sem.at[0])
    load_s = pltpu.make_async_copy(source_hbm, source, load_sem.at[1])
    load_v.start()
    load_s.start()

    barrier = pltpu.get_barrier_semaphore()

    def greet_plane(i, carry):
        pl.semaphore_signal(barrier, inc=1, device_id=plane_dev(lax.rem(plane + i, 16)), device_id_type=MESH)
        return carry

    def greet_line(i, carry):
        pl.semaphore_signal(barrier, inc=1, device_id=at(iz=lax.rem(z + i, 8)), device_id_type=MESH)
        return carry

    lax.fori_loop(1, 16, greet_plane, 0)
    lax.fori_loop(1, 8, greet_line, 0)
    pl.semaphore_signal(barrier, inc=1, device_id=sibling, device_id_type=MESH)
    load_v.wait()
    load_s.wait()
    pl.semaphore_wait(barrier, 23)

    def products(pair):
        lanes = slice(pair * 256, pair * 256 + 256)

        def slot(t, acc):
            block = values[meta[t]]
            rows = source[meta[CAP + t], :, lanes]
            prod = lax.dot_general(block, rows, (((0,), (0,)), ((), ())), preferred_element_type=F32)
            acc = jnp.where(meta[2 * CAP + t] == 1, prod, acc + prod)
            run[t] = acc.astype(BF16)
            return acc

        lax.fori_loop(0, CAP, slot, jnp.zeros((EDGE, 256), F32), unroll=4)

        def place(i, carry):
            u, v, zz, p = i // 24, lax.rem(i // 6, 4), lax.rem(i // 3, 2), lax.rem(i, 3)
            for side in (0, 1):
                b = (((u * 2 + zz) * 4 + v) if side == 0 else ((v * 2 + zz) * 4 + u)) * PER + p
                end = meta[3 * CAP + b]
                got = run[jnp.maximum(end, 0), :, side * 128:side * 128 + 128]
                part[pair * 2 + side, i] = jnp.where(end >= 0, got, jnp.zeros_like(got))
            return carry

        lax.fori_loop(0, COLS, place, 0, unroll=2)

    def ring(j, stage):
        side = (j + stage) % 2
        u = x if side == 0 else y
        n = 24 if stage == 0 else 6
        h = n // 2
        src = part.at[j] if stage == 0 else mid.at[j]
        one = ring1.at[j] if stage == 0 else ring3.at[j]
        two = ring2.at[j] if stage == 0 else ring4.at[j]
        right, left, far = lax.rem(u + 1, 4), lax.rem(u + 3, 4), lax.rem(u + 2, 4)
        dev = (lambda k: at(ix=k)) if side == 0 else (lambda k: at(iy=k))

        def copy(k, a, b, to):
            return pltpu.make_async_remote_copy(
                src_ref=a, dst_ref=b, send_sem=ring_send.at[j, stage, k], recv_sem=ring_recv.at[j, stage, k],
                device_id=dev(to), device_id_type=MESH,
            )

        c = [
            copy(0, src.at[pl.ds(far * n, h)], one.at[0], right),
            copy(1, src.at[pl.ds(far * n + h, h)], one.at[1], left),
            copy(2, src.at[pl.ds(right * n + h, h)], two.at[0, pl.ds(h, h)], right),
            copy(3, src.at[pl.ds(left * n, h)], two.at[1, pl.ds(0, h)], left),
            copy(4, one.at[0], two.at[0, pl.ds(0, h)], right),
            copy(5, one.at[1], two.at[1, pl.ds(h, h)], left),
        ]

        def first():
            for k in range(4):
                c[k].start()

        def second():
            for k, base in ((0, right * n), (1, left * n + h)):
                c[k].wait_recv()

                def add(i, carry):
                    one[k, i] = (one[k, i].astype(F32) + src[base + i].astype(F32)).astype(BF16)
                    return carry

                lax.fori_loop(0, h, add, 0)
                c[4 + k].start()

        def third(write):
            for k in range(2, 6):
                c[k].wait_recv()

            def add(i, carry):
                write(i, src[u * n + i].astype(F32) + two[0, i].astype(F32) + two[1, i].astype(F32))
                return carry

            lax.fori_loop(0, n, add, 0)

        def drain():
            for k in range(6):
                c[k].wait_send()

        return first, second, third, drain

    rings = {(j, s): ring(j, s) for j in range(PARTS) for s in (0, 1)}
    z_copy = [
        pltpu.make_async_remote_copy(
            src_ref=last_sum.at[j, pl.ds((1 - z_lo) * PER, PER)], dst_ref=z_in.at[j],
            send_sem=z_send.at[j], recv_sem=z_recv.at[j],
            device_id=at(iz=z_hi * 2 + 1 - z_lo), device_id_type=MESH,
        )
        for j in range(PARTS)
    ]

    for pair in (0, 1):
        products(pair)
        rings[2 * pair, 0][0]()
        rings[2 * pair + 1, 0][0]()
    for j in range(PARTS):
        rings[j, 0][1]()
    for j in range(PARTS):
        def to_mid(i, v, j=j):
            mid[j, i] = v.astype(BF16)
        rings[j, 0][2](to_mid)
        rings[j, 1][0]()
    for j in range(PARTS):
        rings[j, 1][1]()
    for j in range(PARTS):
        def to_last(i, v, j=j):
            last_sum[j, i] = v.astype(BF16)
        rings[j, 1][2](to_last)
        z_copy[j].start()
    for j in range(PARTS):
        z_copy[j].wait_recv()
        for p in range(PER):
            total = last_sum[j, z_lo * PER + p].astype(F32) + z_in[j, p].astype(F32)
            agg[p * 128:p * 128 + 128, j * 128:j * 128 + 128] = (total * scale[p * 128:p * 128 + 128, :]).astype(BF16)

    def weight_half(which, dst):
        f = features[:, pl.ds(pl.multiple_of(which * 256, 256), 256)]
        for j in range(PARTS):
            d = lax.dot_general(f, agg[:, j * 128:j * 128 + 128], (((0,), (0,)), ((), ())), preferred_element_type=F32)
            for q in range(4):
                dst[j * 4 + q] = d[q * 64:q * 64 + 64, :]

    def remote(src, dst, ss, rs, to):
        return pltpu.make_async_remote_copy(
            src_ref=src, dst_ref=dst, send_sem=ss, recv_sem=rs, device_id=to, device_id_type=MESH
        )

    weight_half(1 - core, w_send)
    give = remote(w_send, w_in, sib_send.at[0], sib_recv.at[0], sibling)
    give.start()
    weight_half(core, w_own)
    give.wait_recv()
    for p in range(16):
        w_own[p] = w_own[p] + w_in[p]

    def all_to_all(count, me, dev, copy_of):
        def go(i, carry):
            to = lax.rem(me + i, count)
            copy_of(to, me, dev(to)).start()
            return carry

        def arrive(i, carry):
            frm = lax.rem(me + i, count)
            copy_of(me, frm, dev(frm)).wait_recv()
            return carry

        def drain(i, carry):
            to = lax.rem(me + i, count)
            copy_of(to, me, dev(to)).wait_send()
            return carry

        return (
            lambda: lax.fori_loop(1, count, go, 0),
            lambda: lax.fori_loop(1, count, arrive, 0),
            lambda: lax.fori_loop(1, count, drain, 0),
        )

    def line_dev(k):
        return at(iz=k)

    plane_go, plane_arrive, plane_drain = all_to_all(16, plane, plane_dev, lambda to, frm, d: remote(
        w_own.at[to], w_plane.at[frm], plane_send.at[0, to], plane_recv.at[0, frm], d))
    line_go, line_arrive, line_drain = all_to_all(8, z, line_dev, lambda to, frm, d: remote(
        w_piece.at[to], w_line.at[frm], line_send.at[0, to], line_recv.at[0, frm], d))
    line_go2, line_arrive2, line_drain2 = all_to_all(8, z, line_dev, lambda to, frm, d: remote(
        w_z.at[z], w_z.at[frm], line_send.at[1, to], line_recv.at[1, frm], d))
    plane_go2, plane_arrive2, plane_drain2 = all_to_all(16, plane, plane_dev, lambda to, frm, d: remote(
        w_full.at[plane], w_full.at[frm], plane_send.at[1, to], plane_recv.at[1, frm], d))

    plane_go()
    out_features[...] = lax.dot_general(
        agg[...], weight[...], (((1,), (1,)), ((), ())), preferred_element_type=F32
    ).astype(BF16)
    w_plane[plane] = w_own[plane]
    plane_arrive()
    total = w_plane[0]
    for p in range(1, 16):
        total = total + w_plane[p]
    for k in range(8):
        w_piece[k] = total[k * 8:k * 8 + 8, :]
    line_go()
    w_line[z] = w_piece[z]
    line_arrive()
    total = w_line[0]
    for k in range(1, 8):
        total = total + w_line[k]
    w_z[z] = total
    line_go2()
    line_arrive2()
    for k in range(8):
        w_full[plane, k * 8:k * 8 + 8, :] = w_z[k]
    plane_go2()
    plane_arrive2()
    back = remote(w_full, w_sib, sib_send.at[1], sib_recv.at[1], sibling)
    back.start()
    mine = pl.multiple_of(core * 256, 256)
    other = pl.multiple_of((1 - core) * 256, 256)
    for j in range(PARTS):
        for q in range(4):
            out_weight[pl.ds(mine + q * 64, 64), j * 128:j * 128 + 128] = w_full[j * 4 + q]
    back.wait_recv()
    for j in range(PARTS):
        for q in range(4):
            out_weight[pl.ds(other + q * 64, 64), j * 128:j * 128 + 128] = w_sib[j * 4 + q]

    for key in rings:
        rings[key][3]()
    for j in range(PARTS):
        z_copy[j].wait_send()
    give.wait_send()
    back.wait_send()
    plane_drain()
    line_drain()
    line_drain2()
    plane_drain2()


def slot_table(coords, count):
    index = jnp.arange(CAP, dtype=jnp.int32)
    live = index < count
    rows, cols = coords[:, 0], coords[:, 1]
    key = jnp.where(live, cols * 32 + rows, 4096 + index)
    rank = jnp.sum((key[None, :] < key[:, None]).astype(jnp.int32), axis=1)
    hit = rank[None, :] == index[:, None]
    pick = lambda v: jnp.sum(jnp.where(hit, v[None, :], 0), axis=1)
    first = jnp.ones((CAP,), jnp.int32)
    order, srow, scol = pick(index), pick(rows), pick(cols)
    first = jnp.concatenate([first[:1], (scol[1:] != scol[:-1]).astype(jnp.int32)])
    lanes = jnp.arange(COLS, dtype=jnp.int32)[:, None]
    upto = jnp.sum((live & (cols <= lanes)).astype(jnp.int32), axis=1)
    has = jnp.any(live & (cols == lanes), axis=1)
    end = jnp.where(has, upto - 1, -1)
    return jnp.concatenate([order, srow, first, end, jnp.zeros((CAP - COLS,), jnp.int32)])


def body(grad_out, features, weight, degrees, block_coords, block_values, block_counts):
    inv_root = lax.rsqrt(degrees.astype(F32))
    scaled = (grad_out.astype(F32) * inv_root[:, None]).astype(BF16)
    gathered = lax.all_gather(scaled, "row", axis=0, tiled=True).reshape(24, EDGE, 512)
    meta = slot_table(block_coords[0, 0], block_counts[0, 0])
    scale = jnp.broadcast_to(inv_root[:, None], (384, 128))
    vm = lambda *s: pltpu.VMEM(s, BF16)
    vf = lambda *s: pltpu.VMEM(s, F32)
    dma = lambda *s: pltpu.SemaphoreType.DMA(s)
    any_spec, vmem_spec = pl.BlockSpec(memory_space=pl.ANY), pl.BlockSpec(memory_space=pltpu.VMEM)
    return pl.pallas_call(
        fused,
        out_shape=(jax.ShapeDtypeStruct((384, 512), BF16), jax.ShapeDtypeStruct((512, 512), F32)),
        in_specs=[pl.BlockSpec(memory_space=pltpu.SMEM), any_spec, any_spec, vmem_spec, vmem_spec, vmem_spec],
        out_specs=(vmem_spec, vmem_spec),
        scratch_shapes=[
            vm(CAP, EDGE, EDGE), vm(24, EDGE, 512), vm(CAP, EDGE, 256), vm(PARTS, COLS, EDGE, EDGE),
            vm(PARTS, 2, 12, EDGE, EDGE), vm(PARTS, 2, 24, EDGE, EDGE), vm(PARTS, 24, EDGE, EDGE),
            vm(PARTS, 2, 3, EDGE, EDGE), vm(PARTS, 2, 6, EDGE, EDGE), vm(PARTS, 6, EDGE, EDGE),
            vm(PARTS, PER, EDGE, EDGE), vm(384, 512),
            vf(16, 64, 128), vf(16, 64, 128), vf(16, 64, 128), vf(16, 64, 128), vf(8, 8, 128), vf(8, 8, 128),
            vf(8, 8, 128), vf(16, 64, 128), vf(16, 64, 128),
            dma(2), dma(PARTS, 2, 6), dma(PARTS, 2, 6), dma(PARTS), dma(PARTS), dma(2), dma(2),
            dma(2, 16), dma(2, 16), dma(2, 8), dma(2, 8),
        ],
        compiler_params=pltpu.CompilerParams(
            collective_id=0, has_side_effects=True, vmem_limit_bytes=60 * 1024 * 1024
        ),
    )(meta, block_values[0, 0], gathered, scale, features, weight)


def solution(mesh):
    in_specs = (
        P(("row", "col"), None),
        P(("row", "col"), None),
        P(),
        P(("row", "col")),
        P("row", "col", None, None),
        P("row", "col", None, None, None),
        P("row", "col"),
    )
    out_specs = (P(("row", "col"), None), P())
    return jax.shard_map(body, mesh=mesh, in_specs=in_specs, out_specs=out_specs, check_vma=False)
```

time: 698 us -> 199 us (0.29)
  waiting for transfers between devices: 576 us -> 46.4 us
  Pallas kernels: 0 us -> 128 us
  other arithmetic: 55 us -> 4.07 us
  local copies, waits for them, and re-layouts: 31.7 us -> 5.49 us
  matrix products: 18.6 us -> 0 us
    psum x1 -> x0, waiting for transfers between devices: 274 us -> none  [body(): grad_weight = lax.psum(local_weight, ('row', 'col'))]
    reduce_scatter x1 -> x0, waiting for transfers between devices: 263 us -> none  [body(): lax.psum_scatter(finished.reshape(out_blocks * block_edge, feat_width).as...]
    pallas_call x0 -> x1, Pallas kernels: none -> 128 us  [body(): pl.pallas_call(fused, out_shape=(jax.ShapeDtypeStruct((384, 512), BF16),...]
    scatter-add x2 -> x0, other arithmetic: 37.7 us -> none  [accumulate(): return partial_acc.at[slot_pair[:, 1]].add(contribution)]
    dot_general x4 -> x0, matrix products: 18.6 us -> none  [the longest x2 13.9 us: accumulate(): jnp.einsum('sab,saf->sbf', slot_blocks, picked, preferred_element_type=jn...]
    convert_element_type x2, other arithmetic: 15.2 us -> 1.96 us  [the longest x1 1.89 us: body(): scaled = (grad_out.astype(F32) * inv_root[:, None]).astype(BF16)]
    broadcast_in_dim x1 -> x2, local copies, waits for them, and re-layouts: 11.5 us -> 0.79 us  [the longest x1 0.79 us: body(): scale = jnp.broadcast_to(inv_root[:, None], (384, 128))]
    gather x2 -> x0, local copies, waits for them, and re-layouts: 9.35 us -> none  [accumulate(): picked = source[slot_pair[:, 0], :, 0:0 + feat_width]]
  transfers between devices with their start and end apart: 3 -> 1, of which waited for: 3 -> 1; matrix products, arithmetic and copies ran while one was open for 1% -> 1% of each run, Pallas kernels for 0% -> 0%
where the time goes in v1:
time: 199 us; the launch traced here: 198 us
  Pallas kernels  128 us (64%)
  waiting for transfers between devices  46.4 us (23%)
  between operations  14.7 us (7%)
  local copies, waits for them, and re-layouts  5.49 us (3%)
  other arithmetic  4.07 us (2%)
    pallas_call x1, Pallas kernels, body(): pl.pallas_call(fused, out_shape=(jax.ShapeDtypeStruct((384, 512), BF16),...  128 us
    all_gather x1, waiting for transfers between devices, body(): lax.all_gather(scaled, 'row', axis=0, tiled=True).reshape(24, EDGE, 512)  46.4 us
    unnamed x2, local copies, waits for them, and re-layouts  4.03 us
  transfers between devices with their start and end apart: 1, of which 1 were waited for; matrix products, arithmetic and copies ran while one was open for 1% of the time, Pallas kernels for 0%

profile of v1, /device:TPU:1, one launch (start us, length us, event | category | flops | bytes accessed | tf_op | source)
XLA Modules:
  0.0 198.2 jit_solution(8087037497960353981)
XLA Ops:
  7.2 0.0 all-gather.2.cloned.1.call-start
  7.2 0.7 convert_rsqrt_fusion
  7.9 1.9 multiply_convert_fusion
  9.8 0.0 all-gather.2.cloned.1.call-update
  10.5 0.8 compare_select_fusion
  11.2 0.2 convert_reduce_fusion
  11.4 0.1 convert_reduce_fusion.1
  11.6 0.1 fusion.1
  11.7 0.2 select_reduce_fusion
  11.9 0.1 compare_convert_fusion
  12.0 0.7 concatenate.3.meta
  12.6 46.4 %all-gather.2.cloned.1.call-done = bf16[3072,512]{1,0:T(8,128)(2,1)} async-done(((bf16[384,512]{1,0:T(8,128)(2,1)}), bf16[3072,512]{1,0:T(8,128)(2,1)}) %all-gather.2.cloned.1.call-update) | async-done | bytes 3145744 | tf_op jit(solution)/shard_map/all_gather | solution.py:302
  59.0 0.8 broadcast_in_dim.49.scale
  59.8 127.5 %shard_map.86 = (bf16[384,512]{1,0:T(8,128)(2,1)}, f32[512,512]{1,0:T(8,128)}) custom-call(s32[640]{0:T(1024)} %concatenate.3.meta, bf16[160,128,128]{2,1,0:T(8,128)(2,1)} %bitcast.10, bf16[24,128,512]{2,1,0:T(8,128)(2,1)} %bitcast.11, f32[384,128]{1,0:T(8,128)} %broadcast_in_dim.49.scale, bf16[384,512]{1,0:T(8,128)(2,1)} %features.1, bf16[512,512]{1,0:T(8,128)(2,1)} %weight.1), custom_call_target="tpu_custom_call" | custom-call | tf_op jit(solution)/shard_map/pallas_call | solution.py:309
  187.4 1.8 copy.12
  189.1 2.3 %copy.13 = f32[512,512]{1,0:T(8,128)} copy(f32[512,512]{1,0:T(8,128)} %get-tuple-element.11) | data formatting | bytes 2097152
  (4 shorter events, 0.0 us)
Async XLA Ops:
  7.2 51.8 %all-gather.2.cloned.1.call-start = ((), (), s32[]{:S(2)}) async-start(), calls=%async_computation | async-start | bytes 3538944 | tf_op jit(solution)/shard_map/all_gather | solution.py:302
Sparse Core Ops, SparseCore 0:
  10.4 48.5 all-gather.1

commit v2 on v1

v2 whole, which is shorter than its diff:
```python
import functools

import jax
import jax.numpy as jnp
from jax import lax
from jax.experimental import pallas as pl
from jax.experimental.pallas import tpu as pltpu
from jax.sharding import PartitionSpec as P

MESH = pl.DeviceIdType.MESH
F32, BF16 = jnp.float32, jnp.bfloat16
CAP = 160
EDGE = 128
COLS = 96
PER = 3
PARTS = 4
UNROLL = 16


def fused(
    meta, values_hbm, grad_out, scale, features, weight,
    out_features, out_weight,
    values, source0, source1, source2, source3, run, part, ring1, ring2, mid, ring3, ring4, last_sum, z_in, agg,
    w_send, w_own, w_in, w_out, w_plane, w_line, w_full, w_sib,
    load_sem, get_send, get_recv, ring_send, ring_recv, z_send, z_recv, sib_send, sib_recv,
    plane_send, plane_recv, line_send, line_recv,
):
    row, col = lax.axis_index("row"), lax.axis_index("col")
    core = lax.rem(row, 2)
    z_hi = row // 2
    x, z_lo, y = col // 8, lax.rem(col // 4, 2), lax.rem(col, 4)
    z = z_hi * 2 + z_lo
    plane = x * 4 + y

    def at(ix=x, iz=z, iy=y, icore=core):
        return ((iz // 2) * 2 + icore, (ix * 2 + lax.rem(iz, 2)) * 4 + iy)

    def plane_dev(p):
        return at(ix=p // 4, iy=lax.rem(p, 4))

    def line_dev(k):
        return at(iz=k)

    def remote(src, dst, ss, rs, to):
        return pltpu.make_async_remote_copy(
            src_ref=src, dst_ref=dst, send_sem=ss, recv_sem=rs, device_id=to, device_id_type=MESH
        )

    sibling = at(icore=1 - core)
    source = (source0, source1, source2, source3)

    load_v = pltpu.make_async_copy(values_hbm, values, load_sem)
    load_v.start()

    barrier = pltpu.get_barrier_semaphore()

    def greet_plane(i, carry):
        pl.semaphore_signal(barrier, inc=1, device_id=plane_dev(lax.rem(plane + i, 16)), device_id_type=MESH)
        return carry

    def greet_line(i, carry):
        pl.semaphore_signal(barrier, inc=1, device_id=line_dev(lax.rem(z + i, 8)), device_id_type=MESH)
        return carry

    lax.fori_loop(1, 16, greet_plane, 0)
    lax.fori_loop(1, 8, greet_line, 0)
    pl.semaphore_signal(barrier, inc=1, device_id=sibling, device_id_type=MESH)

    for j in range(PARTS):
        for p in range(PER):
            got = grad_out[p * 128:p * 128 + 128, j * 128:j * 128 + 128].astype(F32)
            source[j][row * PER + p] = (got * scale[p * 128:p * 128 + 128, :]).astype(BF16)

    pl.semaphore_wait(barrier, 23)

    def gather(j):
        up, down, far = lax.rem(z_hi + 1, 4), lax.rem(z_hi + 3, 4), lax.rem(z_hi + 2, 4)
        dev = lambda h: (h * 2 + core, col)
        cut = 1 + j % 2

        def copy(k, zh, to, start=0, size=PER):
            ref = source[j].at[pl.ds((zh * 2 + core) * PER + start, size)]
            return remote(ref, ref, get_send.at[j, k], get_recv.at[j, k], to)

        own_up, own_down, own_sib = copy(0, z_hi, dev(up)), copy(1, z_hi, dev(down)), copy(2, z_hi, sibling)
        fwd_up = copy(3, down, dev(up), 0, cut)
        fwd_down = copy(4, up, dev(down), cut, PER - cut)
        sib_down, sib_up = copy(5, down, sibling), copy(6, up, sibling)
        sib_far = copy(7, far, sibling)

        def own():
            own_up.start()
            own_down.start()
            own_sib.start()

        def forward():
            own_up.wait_recv()
            fwd_up.start()
            own_down.wait_recv()
            fwd_down.start()
            sib_down.start()
            sib_up.start()

        def finish():
            fwd_up.wait_recv()
            fwd_down.wait_recv()
            sib_far.start()
            own_sib.wait_recv()
            sib_down.wait_recv()
            sib_up.wait_recv()
            sib_far.wait_recv()

        def drain():
            for c in (own_up, own_down, own_sib, fwd_up, fwd_down, sib_down, sib_up, sib_far):
                c.wait_send()

        return own, forward, finish, drain

    gathers = [gather(j) for j in range(PARTS)]

    def products(j):
        def slot(t, acc):
            prod = lax.dot_general(
                values[meta[t]], source[j][meta[CAP + t]], (((0,), (0,)), ((), ())), preferred_element_type=F32
            )
            acc = jnp.where(meta[2 * CAP + t] == 1, prod, acc + prod)
            run[t] = acc.astype(BF16)
            return acc

        lax.fori_loop(0, CAP, slot, jnp.zeros((EDGE, EDGE), F32), unroll=UNROLL)

        def place(i, carry):
            u, v, zz, p = i // 24, lax.rem(i // 6, 4), lax.rem(i // 3, 2), lax.rem(i, 3)
            b = (((u * 2 + zz) * 4 + v) if j % 2 == 0 else ((v * 2 + zz) * 4 + u)) * PER + p
            end = meta[3 * CAP + b]
            got = run[jnp.maximum(end, 0)]
            part[j, i] = jnp.where(end >= 0, got, jnp.zeros_like(got))
            return carry

        lax.fori_loop(0, COLS, place, 0, unroll=4)

    def ring(j, stage):
        side = (j + stage) % 2
        u = x if side == 0 else y
        n = 24 if stage == 0 else 6
        h = n // 2
        src = part.at[j] if stage == 0 else mid.at[j]
        one = ring1.at[j] if stage == 0 else ring3.at[j]
        two = ring2.at[j] if stage == 0 else ring4.at[j]
        right, left, far = lax.rem(u + 1, 4), lax.rem(u + 3, 4), lax.rem(u + 2, 4)
        dev = (lambda k: at(ix=k)) if side == 0 else (lambda k: at(iy=k))

        def copy(k, a, b, to):
            return remote(a, b, ring_send.at[j, stage, k], ring_recv.at[j, stage, k], dev(to))

        c = [
            copy(0, src.at[pl.ds(far * n, h)], one.at[0], right),
            copy(1, src.at[pl.ds(far * n + h, h)], one.at[1], left),
            copy(2, src.at[pl.ds(right * n + h, h)], two.at[0, pl.ds(h, h)], right),
            copy(3, src.at[pl.ds(left * n, h)], two.at[1, pl.ds(0, h)], left),
            copy(4, one.at[0], two.at[0, pl.ds(0, h)], right),
            copy(5, one.at[1], two.at[1, pl.ds(h, h)], left),
        ]

        def first():
            for k in range(4):
                c[k].start()

        def second():
            for k, base in ((0, right * n), (1, left * n + h)):
                c[k].wait_recv()

                def add(i, carry):
                    one[k, i] = (one[k, i].astype(F32) + src[base + i].astype(F32)).astype(BF16)
                    return carry

                lax.fori_loop(0, h, add, 0)
                c[4 + k].start()

        def third():
            for k in range(2, 6):
                c[k].wait_recv()
            dst = mid if stage == 0 else last_sum

            def add(i, carry):
                v = src[u * n + i].astype(F32) + two[0, i].astype(F32) + two[1, i].astype(F32)
                dst[j, i] = v.astype(BF16)
                return carry

            lax.fori_loop(0, n, add, 0)

        def drain():
            for k in range(6):
                c[k].wait_send()

        return first, second, third, drain

    rings = {(j, s): ring(j, s) for j in range(PARTS) for s in (0, 1)}
    z_copy = [
        remote(
            last_sum.at[j, pl.ds((1 - z_lo) * PER, PER)], z_in.at[j], z_send.at[j], z_recv.at[j],
            at(iz=z_hi * 2 + 1 - z_lo),
        )
        for j in range(PARTS)
    ]

    def r1(j):
        rings[j, 0][0]()

    def r2(j):
        rings[j, 0][1]()

    def r3(j):
        rings[j, 0][2]()
        rings[j, 1][0]()

    def r4(j):
        rings[j, 1][1]()

    def r5(j):
        rings[j, 1][2]()
        z_copy[j].start()

    def r6(j):
        z_copy[j].wait_recv()
        for p in range(PER):
            total = last_sum[j, z_lo * PER + p].astype(F32) + z_in[j, p].astype(F32)
            agg[p * 128:p * 128 + 128, j * 128:j * 128 + 128] = (total * scale[p * 128:p * 128 + 128, :]).astype(BF16)

    def all_to_all(count, me, dev, copy_of):
        def go(i, carry):
            to = lax.rem(me + i, count)
            copy_of(to, me, dev(to)).start()
            return carry

        def arrive(i, carry):
            frm = lax.rem(me + i, count)
            copy_of(me, frm, dev(frm)).wait_recv()
            return carry

        def drain(i, carry):
            to = lax.rem(me + i, count)
            copy_of(to, me, dev(to)).wait_send()
            return carry

        return (
            lambda: lax.fori_loop(1, count, go, 0),
            lambda: lax.fori_loop(1, count, arrive, 0),
            lambda: lax.fori_loop(1, count, drain, 0),
        )

    def weight_sum(g):
        give = remote(w_send.at[g], w_in.at[g], sib_send.at[g, 0], sib_recv.at[g, 0], sibling)
        back = remote(w_full.at[g], w_sib.at[g], sib_send.at[g, 1], sib_recv.at[g, 1], sibling)
        go1, arrive1, drain1 = all_to_all(16, plane, plane_dev, lambda to, frm, d: remote(
            w_out.at[g, to], w_plane.at[g, frm], plane_send.at[g, 0, to], plane_recv.at[g, 0, frm], d))
        go2, arrive2, drain2 = all_to_all(8, z, line_dev, lambda to, frm, d: remote(
            w_line.at[g, z], w_line.at[g, frm], line_send.at[g, to], line_recv.at[g, frm], d))
        go3, arrive3, drain3 = all_to_all(16, plane, plane_dev, lambda to, frm, d: remote(
            w_full.at[g, plane], w_full.at[g, frm], plane_send.at[g, 1, to], plane_recv.at[g, 1, frm], d))

        def half(which, dst):
            f = features[:, pl.ds(pl.multiple_of(which * 256, 256), 256)]
            for k in range(2):
                lanes = slice((g * 2 + k) * 128, (g * 2 + k) * 128 + 128)
                d = lax.dot_general(f, agg[:, lanes], (((0,), (0,)), ((), ())), preferred_element_type=F32)
                for q in range(8):
                    dst[g, k * 8 + q] = d[q * 32:q * 32 + 32, :].astype(dst.dtype)

        def a():
            half(1 - core, w_send)
            give.start()
            half(core, w_own)

        def b():
            give.wait_recv()
            for p in range(16):
                w_out[g, p] = (w_own[g, p] + w_in[g, p].astype(F32)).astype(BF16)
            go1()
            w_plane[g, plane] = w_out[g, plane]

        def c():
            arrive1()
            total = w_plane[g, 0].astype(F32)
            for p in range(1, 16):
                total = total + w_plane[g, p].astype(F32)
            w_line[g, z] = total.astype(BF16)
            go2()

        def d():
            arrive2()
            total = w_line[g, 0].astype(F32)
            for k in range(1, 8):
                total = total + w_line[g, k].astype(F32)
            w_full[g, plane] = total.astype(BF16)
            go3()

        def write(which, src):
            base = pl.multiple_of(which * 256, 256)
            for k in range(2):
                for q in range(8):
                    out_weight[pl.ds(base + q * 32, 32), (g * 2 + k) * 128:(g * 2 + k) * 128 + 128] = (
                        src[g, k * 8 + q].astype(F32)
                    )

        def e():
            arrive3()
            back.start()
            write(core, w_full)

        def f():
            back.wait_recv()
            write(1 - core, w_sib)

        def drain():
            give.wait_send()
            back.wait_send()
            drain1()
            drain2()
            drain3()

        return a, b, c, d, e, f, drain

    ws = [weight_sum(g) for g in range(2)]

    gathers[0][0]()
    gathers[1][0]()
    gathers[0][1]()
    gathers[2][0]()
    gathers[0][2]()
    load_v.wait()
    for j in range(PARTS):
        if j + 1 < PARTS:
            gathers[j + 1][1]()
        if j + 3 < PARTS:
            gathers[j + 3][0]()
        products(j)
        r1(j)
        if j + 1 < PARTS:
            gathers[j + 1][2]()
        if j >= 2:
            r2(j - 2)
    r2(2)
    r3(0)
    r2(3)
    r3(1)
    r4(0)
    r3(2)
    r4(1)
    r3(3)
    r5(0)
    r5(1)
    r4(2)
    r4(3)
    r6(0)
    r6(1)
    ws[0][0]()
    r5(2)
    ws[0][1]()
    r5(3)
    ws[0][2]()
    r6(2)
    r6(3)
    ws[1][0]()
    ws[0][3]()
    ws[1][1]()
    out_features[...] = lax.dot_general(
        agg[...], weight[...], (((1,), (1,)), ((), ())), preferred_element_type=F32
    ).astype(BF16)
    ws[0][4]()
    ws[1][2]()
    ws[0][5]()
    ws[1][3]()
    ws[1][4]()
    ws[1][5]()

    for j in range(PARTS):
        gathers[j][3]()
    for key in rings:
        rings[key][3]()
    for j in range(PARTS):
        z_copy[j].wait_send()
    for g in range(2):
        ws[g][6]()


def slot_table(coords, count):
    index = jnp.arange(CAP, dtype=jnp.int32)
    live = index < count
    rows, cols = coords[:, 0], coords[:, 1]
    key = jnp.where(live, cols * 32 + rows, 4096 + index)
    rank = jnp.sum((key[None, :] < key[:, None]).astype(jnp.int32), axis=1)
    hit = rank[None, :] == index[:, None]
    pick = lambda v: jnp.sum(jnp.where(hit, v[None, :], 0), axis=1)
    first = jnp.ones((CAP,), jnp.int32)
    order, srow, scol = pick(index), pick(rows), pick(cols)
    first = jnp.concatenate([first[:1], (scol[1:] != scol[:-1]).astype(jnp.int32)])
    lanes = jnp.arange(COLS, dtype=jnp.int32)[:, None]
    upto = jnp.sum((live & (cols <= lanes)).astype(jnp.int32), axis=1)
    has = jnp.any(live & (cols == lanes), axis=1)
    end = jnp.where(has, upto - 1, -1)
    return jnp.concatenate([order, srow, first, end, jnp.zeros((CAP - COLS,), jnp.int32)])


def body(grad_out, features, weight, degrees, block_coords, block_values, block_counts):
    meta = slot_table(block_coords[0, 0], block_counts[0, 0])
    scale = lax.rsqrt(jnp.broadcast_to(degrees[:, None], (384, 128)).astype(F32))
    vm = lambda *s: pltpu.VMEM(s, BF16)
    vf = lambda *s: pltpu.VMEM(s, F32)
    dma = lambda *s: pltpu.SemaphoreType.DMA(s)
    any_spec, vmem_spec = pl.BlockSpec(memory_space=pl.ANY), pl.BlockSpec(memory_space=pltpu.VMEM)
    return pl.pallas_call(
        fused,
        out_shape=(jax.ShapeDtypeStruct((384, 512), BF16), jax.ShapeDtypeStruct((512, 512), F32)),
        in_specs=[pl.BlockSpec(memory_space=pltpu.SMEM), any_spec, vmem_spec, vmem_spec, vmem_spec, vmem_spec],
        out_specs=(vmem_spec, vmem_spec),
        scratch_shapes=[
            vm(CAP, EDGE, EDGE), vm(24, EDGE, EDGE), vm(24, EDGE, EDGE), vm(24, EDGE, EDGE), vm(24, EDGE, EDGE), vm(CAP, EDGE, EDGE), vm(PARTS, COLS, EDGE, EDGE),
            vm(PARTS, 2, 12, EDGE, EDGE), vm(PARTS, 2, 24, EDGE, EDGE), vm(PARTS, 24, EDGE, EDGE),
            vm(PARTS, 2, 3, EDGE, EDGE), vm(PARTS, 2, 6, EDGE, EDGE), vm(PARTS, 6, EDGE, EDGE),
            vm(PARTS, PER, EDGE, EDGE), vm(384, 512),
            vm(2, 16, 32, 128), vf(2, 16, 32, 128), vm(2, 16, 32, 128), vm(2, 16, 32, 128), vm(2, 16, 32, 128),
            vm(2, 8, 32, 128), vm(2, 16, 32, 128), vm(2, 16, 32, 128),
            pltpu.SemaphoreType.DMA, dma(PARTS, 8), dma(PARTS, 8), dma(PARTS, 2, 6), dma(PARTS, 2, 6),
            dma(PARTS), dma(PARTS), dma(2, 2), dma(2, 2),
            dma(2, 2, 16), dma(2, 2, 16), dma(2, 8), dma(2, 8),
        ],
        compiler_params=pltpu.CompilerParams(
            collective_id=0, has_side_effects=True, vmem_limit_bytes=60 * 1024 * 1024
        ),
    )(meta, block_values[0, 0], grad_out, scale, features, weight)


def solution(mesh):
    in_specs = (
        P(("row", "col"), None),
        P(("row", "col"), None),
        P(),
        P(("row", "col")),
        P("row", "col", None, None),
        P("row", "col", None, None, None),
        P("row", "col"),
    )
    out_specs = (P(("row", "col"), None), P())
    return jax.shard_map(body, mesh=mesh, in_specs=in_specs, out_specs=out_specs, check_vma=False)
```

time: 199 us -> 152 us (0.76)
  waiting for transfers between devices: 46.4 us -> 0 us
  Pallas kernels: 128 us -> 143 us
  between operations: 14.7 us -> 1.3 us
    all_gather x1 -> x0, waiting for transfers between devices: 46.4 us -> none  [body(): lax.all_gather(scaled, 'row', axis=0, tiled=True).reshape(24, EDGE, 512)]
    pallas_call x1, Pallas kernels: 128 us -> 143 us  [body(): pl.pallas_call(fused, out_shape=(jax.ShapeDtypeStruct((384, 512), BF16),...]
  transfers between devices with their start and end apart: 1 -> 0, of which waited for: 1 -> 0; matrix products, arithmetic and copies ran while one was open for 1% -> 0% of each run, Pallas kernels for 0% -> 0%
where the time goes in v2:
time: 152 us
  Pallas kernels  143 us (94%)
  local copies, waits for them, and re-layouts  5.5 us (4%)
  other arithmetic  2.19 us (1%)
    pallas_call x1, Pallas kernels, body(): pl.pallas_call(fused, out_shape=(jax.ShapeDtypeStruct((384, 512), BF16),...  143 us
    unnamed x2, local copies, waits for them, and re-layouts  4.03 us

profile of v2, /device:TPU:1, one launch (start us, length us, event | category | flops | bytes accessed | tf_op | source)
XLA Modules:
  0.0 152.1 jit_solution(17736657882290885293)
XLA Ops:
  1.3 0.7 convert_rsqrt_fusion
  2.0 0.8 compare_select_fusion
  2.8 0.2 convert_reduce_fusion
  2.9 0.1 convert_reduce_fusion.1
  3.1 0.1 fusion.1
  3.2 0.2 select_reduce_fusion
  3.4 0.1 compare_convert_fusion
  3.5 0.7 concatenate.3.meta
  4.2 0.8 broadcast_in_dim.48.scale
  4.9 143.1 %shard_map.86 = (bf16[384,512]{1,0:T(8,128)(2,1)}, f32[512,512]{1,0:T(8,128)}) custom-call(s32[640]{0:T(1024)} %concatenate.3.meta, bf16[160,128,128]{2,1,0:T(8,128)(2,1)} %bitcast.9, bf16[384,512]{1,0:T(8,128)(2,1)} %grad_out.1, f32[384,128]{1,0:T(8,128)} %broadcast_in_dim.48.scale, bf16[384,512]{1,0:T(8,128)(2,1)} %features.1, bf16[512,512]{1,0:T(8,128)(2,1)} %weight.1), custom_call_target="tpu_custom_call" | custom-call | tf_op jit(solution)/shard_map/pallas_call | solution.py:412
  148.0 1.8 %copy.12 = bf16[384,512]{1,0:T(8,128)(2,1)} copy(bf16[384,512]{1,0:T(8,128)(2,1)} %get-tuple-element.10) | data formatting | bytes 786432
  149.8 2.3 %copy.13 = f32[512,512]{1,0:T(8,128)} copy(f32[512,512]{1,0:T(8,128)} %get-tuple-element.11) | data formatting | bytes 2097152
  (4 shorter events, 0.0 us)

commit v3 on v2

v3 whole, which is shorter than its diff:
```python
import functools

import jax
import jax.numpy as jnp
from jax import lax
from jax.experimental import pallas as pl
from jax.experimental.pallas import tpu as pltpu
from jax.sharding import PartitionSpec as P

MESH = pl.DeviceIdType.MESH
F32, BF16 = jnp.float32, jnp.bfloat16
CAP = 160
EDGE = 128
COLS = 96
PER = 3
PARTS = 4
UNROLL = 32
UNROLL_GO = {16: 5, 8: 7}
HALF = 64
LAST = PARTS - 1


def fused(
    slot_of, row_of, opens, last_of, values_hbm, grad_out, degrees, features, weight,
    out_features, out_weight,
    values, source0, source1, source2, source3, run, part, ring1, ring2, mid, ring3, ring4, last_sum, z_in, agg, scale, z_first,
    w_send, w_own, w_in, w_out, w_plane, w_line, w_full, w_sib,
    load_sem, first_send, first_recv, get_send, get_recv, ring_send, ring_recv, z_send, z_recv, sib_send, sib_recv,
    plane_send, plane_recv, line_send, line_recv,
):
    row, col = lax.axis_index("row"), lax.axis_index("col")
    core = lax.rem(row, 2)
    z_hi = row // 2
    x, z_lo, y = col // 8, lax.rem(col // 4, 2), lax.rem(col, 4)
    z = z_hi * 2 + z_lo
    plane = x * 4 + y

    def at(ix=x, iz=z, iy=y, icore=core):
        return ((iz // 2) * 2 + icore, (ix * 2 + lax.rem(iz, 2)) * 4 + iy)

    def plane_dev(p):
        return at(ix=p // 4, iy=lax.rem(p, 4))

    def line_dev(k):
        return at(iz=k)

    def remote(src, dst, ss, rs, to):
        return pltpu.make_async_remote_copy(
            src_ref=src, dst_ref=dst, send_sem=ss, recv_sem=rs, device_id=to, device_id_type=MESH
        )

    sibling = at(icore=1 - core)
    source = (source0, source1, source2, source3)

    load_v = pltpu.make_async_copy(values_hbm, values, load_sem)
    load_v.start()

    barrier = pltpu.get_barrier_semaphore()

    def greet_plane(i, carry):
        pl.semaphore_signal(barrier, inc=1, device_id=plane_dev(lax.rem(plane + i, 16)), device_id_type=MESH)
        return carry

    def greet_line(i, carry):
        pl.semaphore_signal(barrier, inc=1, device_id=line_dev(lax.rem(z + i, 8)), device_id_type=MESH)
        return carry

    lax.fori_loop(1, 16, greet_plane, 0)
    lax.fori_loop(1, 8, greet_line, 0)
    pl.semaphore_signal(barrier, inc=1, device_id=sibling, device_id_type=MESH)

    inv_root = lax.rsqrt(degrees[...].astype(F32))
    for p in range(PER):
        scale[p * 128:p * 128 + 128, :] = jnp.broadcast_to(inv_root[p:p + 1, :], (128, 128)).T
    for j in range(PARTS):
        for p in range(PER):
            got = grad_out[p * 128:p * 128 + 128, j * 128:j * 128 + 128].astype(F32)
            source[j][row * PER + p] = (got * scale[p * 128:p * 128 + 128, :]).astype(BF16)

    pl.semaphore_wait(barrier, 23)

    def gather(j):
        up, down, far = lax.rem(z_hi + 1, 4), lax.rem(z_hi + 3, 4), lax.rem(z_hi + 2, 4)
        dev = lambda h: (h * 2 + core, col)
        cut = 1 + j % 2

        def copy(k, zh, to, start=0, size=PER):
            ref = source[j].at[pl.ds((zh * 2 + core) * PER + start, size)]
            return remote(ref, ref, get_send.at[j, k], get_recv.at[j, k], to)

        own_up, own_down, own_sib = copy(0, z_hi, dev(up)), copy(1, z_hi, dev(down)), copy(2, z_hi, sibling)
        fwd_up = copy(3, down, dev(up), 0, cut)
        fwd_down = copy(4, up, dev(down), cut, PER - cut)
        sib_down, sib_up = copy(5, down, sibling), copy(6, up, sibling)
        sib_far = copy(7, far, sibling)

        def own():
            own_up.start()
            own_down.start()
            own_sib.start()

        def forward():
            own_up.wait_recv()
            fwd_up.start()
            own_down.wait_recv()
            fwd_down.start()
            sib_down.start()
            sib_up.start()

        def finish():
            fwd_up.wait_recv()
            fwd_down.wait_recv()
            sib_far.start()
            own_sib.wait_recv()
            sib_down.wait_recv()
            sib_up.wait_recv()
            sib_far.wait_recv()

        def drain():
            for c in (own_up, own_down, own_sib, fwd_up, fwd_down, sib_down, sib_up, sib_far):
                c.wait_send()

        return own, forward, finish, drain

    gathers = [gather(j) for j in range(PARTS)]

    def products(j):
        def slot(t, acc):
            prod = lax.dot_general(
                values[slot_of[t]], source[j][row_of[t]], (((0,), (0,)), ((), ())), preferred_element_type=F32
            )
            acc = jnp.where(opens[t] == 1, prod, acc + prod)
            run[t] = acc.astype(BF16)
            return acc

        lax.fori_loop(0, CAP, slot, jnp.zeros((EDGE, EDGE), F32), unroll=UNROLL)

        def place(b, carry):
            c, p = b // PER, lax.rem(b, PER)
            cx, cz, cy = c // 8, lax.rem(c // 4, 2), lax.rem(c, 4)
            end = last_of[b]
            got = run[jnp.maximum(end, 0)]
            got = jnp.where(end >= 0, got, jnp.zeros_like(got))
            for d, uv in ((0, cx * 4 + cy), (1, cy * 4 + cx)):
                i = (cz * 16 + uv if j == LAST else uv * 2 + cz) * PER + p
                part[j, d, i] = got[d * HALF:d * HALF + HALF]
            return carry

        lax.fori_loop(0, COLS, place, 0, unroll=4)

    def scaled_sum(j, d, p, total):
        rows = slice(p * 128 + d * HALF, p * 128 + d * HALF + HALF)
        agg[rows, j * 128:j * 128 + 128] = (total * scale[rows, :]).astype(BF16)

    def ring(j, side, stage):
        on_x = (side + stage) % 2 == 0
        u = x if on_x else y
        n = (24, 6)[stage] // (2 if j == LAST else 1)
        h = n // 2 + (side if n % 2 else 0)
        src = mid.at[j, side] if stage else z_first.at[side] if j == LAST else part.at[j, side]
        one = (ring1 if stage == 0 else ring3).at[j, side]
        two = (ring2 if stage == 0 else ring4).at[j, side]
        right, left, far = lax.rem(u + 1, 4), lax.rem(u + 3, 4), lax.rem(u + 2, 4)
        dev = (lambda k: at(ix=k)) if on_x else (lambda k: at(iy=k))

        def copy(k, a, b, to):
            return remote(a, b, ring_send.at[j, side, stage, k], ring_recv.at[j, side, stage, k], dev(to))

        c = [
            copy(0, src.at[pl.ds(far * n, h)], one.at[0, pl.ds(0, h)], right),
            copy(1, src.at[pl.ds(far * n + h, n - h)], one.at[1, pl.ds(0, n - h)], left),
            copy(2, src.at[pl.ds(right * n + h, n - h)], two.at[0, pl.ds(h, n - h)], right),
            copy(3, src.at[pl.ds(left * n, h)], two.at[1, pl.ds(0, h)], left),
            copy(4, one.at[0, pl.ds(0, h)], two.at[0, pl.ds(0, h)], right),
            copy(5, one.at[1, pl.ds(0, n - h)], two.at[1, pl.ds(h, n - h)], left),
        ]

        def second(k):
            base, count = ((right * n, h), (left * n + h, n - h))[k]
            wide = 3 if count % 3 == 0 else count
            c[k].wait_recv()

            def add(i, carry):
                at3, from3 = pl.ds(i * wide, wide), pl.ds(base + i * wide, wide)
                one[k, at3] = (one[k, at3].astype(F32) + src[from3].astype(F32)).astype(BF16)
                return carry

            lax.fori_loop(0, count // wide, add, 0)
            c[4 + k].start()

        def third():
            for k in range(2, 6):
                c[k].wait_recv()

            def add(i, carry):
                at3 = pl.ds(i * 3, 3)
                v = src[pl.ds(u * n + i * 3, 3)].astype(F32) + two[0, at3].astype(F32) + two[1, at3].astype(F32)
                if stage == 0:
                    mid[j, side, at3] = v.astype(BF16)
                elif j == LAST:
                    for p in range(PER):
                        scaled_sum(j, side, p, v[p])
                else:
                    last_sum[j, i, side] = v.astype(BF16)
                return carry

            lax.fori_loop(0, n // 3, add, 0)

        return c, second, third

    rings = {(j, d, s): ring(j, d, s) for j in range(PARTS) for d in (0, 1) for s in (0, 1)}
    z_copy = [
        remote(last_sum.at[j, 1 - z_lo], z_in.at[j], z_send.at[j], z_recv.at[j], at(iz=z_hi * 2 + 1 - z_lo))
        for j in range(LAST)
    ]

    def swap(d, k):
        u = lax.rem((x, y)[d] + k, 4)
        cut = pl.ds(u * 12, 12)
        c = remote(
            part.at[LAST, d, pl.ds((1 - z_lo) * 48 + u * 12, 12)], z_first.at[d, cut], first_send.at[d, k],
            first_recv.at[d, k], at(iz=z_hi * 2 + 1 - z_lo),
        )

        def take():
            c.wait_recv()

            def add(i, carry):
                at3 = pl.ds(u * 12 + i * 3, 3)
                own_part = part[LAST, d, pl.ds(z_lo * 48 + u * 12 + i * 3, 3)]
                z_first[d, at3] = (z_first[d, at3].astype(F32) + own_part.astype(F32)).astype(BF16)
                return carry

            lax.fori_loop(0, 4, add, 0)

        return c, take

    swaps = {(d, k): swap(d, k) for d in (0, 1) for k in range(4)}

    def give_z(k):
        for d in (0, 1):
            swaps[d, k][0].start()

    def take_z(k):
        for d in (0, 1):
            swaps[d, k][1]()

    def r1(j, which=(0, 1, 2, 3), stage=0):
        for k in which:
            for d in (0, 1):
                rings[j, d, stage][0][k].start()

    def r2(j, stage=0):
        for k in (0, 1):
            for d in (0, 1):
                rings[j, d, stage][1](k)

    def r3(j):
        for d in (0, 1):
            rings[j, d, 0][2]()
            for k in range(4):
                rings[j, d, 1][0][k].start()

    def r4(j):
        r2(j, 1)

    def r5(j):
        for d in (0, 1):
            rings[j, d, 1][2]()
        if j < LAST:
            z_copy[j].start()

    def r6(j):
        z_copy[j].wait_recv()
        for p in range(PER):
            for d in (0, 1):
                scaled_sum(j, d, p, last_sum[j, z_lo, d, p].astype(F32) + z_in[j, d, p].astype(F32))

    def exchange(count, me, dev, src_of, dst, ss, rs):
        def go(i, carry):
            to = lax.rem(me + i, count)
            remote(src_of(to), dst.at[me], ss, rs, dev(to)).start()
            return carry

        whole = remote(dst.at[pl.ds(0, count - 1)], dst.at[pl.ds(0, count - 1)], ss, rs, dev(lax.rem(me + 1, count)))
        return lambda: lax.fori_loop(1, count, go, 0, unroll=UNROLL_GO[count]), whole.wait_recv, whole.wait_send

    def weight_sum(g):
        give = remote(w_send.at[g], w_in.at[g], sib_send.at[g, 0], sib_recv.at[g, 0], sibling)
        back = remote(w_full.at[g], w_sib.at[g], sib_send.at[g, 1], sib_recv.at[g, 1], sibling)
        go1, arrive1, drain1 = exchange(
            16, plane, plane_dev, lambda to: w_out.at[g, to], w_plane.at[g], plane_send.at[g, 0], plane_recv.at[g, 0])
        go2, arrive2, drain2 = exchange(
            8, z, line_dev, lambda to: w_line.at[g, z], w_line.at[g], line_send.at[g], line_recv.at[g])
        go3, arrive3, drain3 = exchange(
            16, plane, plane_dev, lambda to: w_full.at[g, plane], w_full.at[g], plane_send.at[g, 1], plane_recv.at[g, 1])

        def half(which, dst):
            f = features[:, pl.ds(pl.multiple_of(which * 256, 256), 256)]
            for k in range(2):
                lanes = slice((g * 2 + k) * 128, (g * 2 + k) * 128 + 128)
                d = lax.dot_general(f, agg[:, lanes], (((0,), (0,)), ((), ())), preferred_element_type=F32)
                for q in range(8):
                    dst[g, k * 8 + q] = d[q * 32:q * 32 + 32, :].astype(dst.dtype)

        def a():
            half(1 - core, w_send)
            give.start()
            half(core, w_own)

        def b():
            give.wait_recv()
            for p in range(16):
                w_out[g, p] = (w_own[g, p] + w_in[g, p].astype(F32)).astype(BF16)
            go1()
            w_plane[g, plane] = w_out[g, plane]

        def c():
            arrive1()
            total = w_plane[g, 0].astype(F32)
            for p in range(1, 16):
                total = total + w_plane[g, p].astype(F32)
            w_line[g, z] = total.astype(BF16)
            go2()

        def d():
            arrive2()
            total = w_line[g, 0].astype(F32)
            for k in range(1, 8):
                total = total + w_line[g, k].astype(F32)
            w_full[g, plane] = total.astype(BF16)
            go3()

        def write(which, src):
            base = pl.multiple_of(which * 256, 256)
            for k in range(2):
                for q in range(8):
                    out_weight[pl.ds(base + q * 32, 32), (g * 2 + k) * 128:(g * 2 + k) * 128 + 128] = (
                        src[g, k * 8 + q].astype(F32)
                    )

        def e():
            arrive3()
            back.start()
            write(core, w_full)

        def f():
            back.wait_recv()
            write(1 - core, w_sib)

        def drain():
            give.wait_send()
            back.wait_send()
            drain1()
            drain2()
            drain3()

        return a, b, c, d, e, f, drain

    ws = [weight_sum(g) for g in range(2)]

    own, forward, finish = [[g[i] for g in gathers] for i in range(3)]
    own[0]()
    own[1]()
    forward[0]()
    own[2]()
    forward[1]()
    own[3]()
    finish[0]()
    load_v.wait()
    products(0)
    r1(0)
    forward[2]()
    finish[1]()
    products(1)
    r2(0)
    r1(1)
    forward[3]()
    finish[2]()
    products(2)
    r3(0)
    finish[3]()
    products(3)
    give_z(2)
    give_z(1)
    give_z(3)
    r2(1)
    r1(2)
    r4(0)
    r5(0)
    r3(1)
    take_z(2)
    r1(3, (0, 1))
    r2(2)
    take_z(1)
    r1(3, (2,))
    r4(1)
    r5(1)
    give_z(0)
    r3(2)
    take_z(3)
    r1(3, (3,))
    r2(3)
    r6(0)
    r6(1)
    ws[0][0]()
    r4(2)
    ws[0][1]()
    r5(2)
    take_z(0)
    r3(3)
    ws[0][2]()
    r4(3)
    r6(2)
    ws[0][3]()
    r5(3)
    ws[1][0]()
    ws[1][1]()
    ws[0][4]()
    out_features[...] = lax.dot_general(
        agg[...], weight[...], (((1,), (1,)), ((), ())), preferred_element_type=F32
    ).astype(BF16)
    for j in range(PARTS):
        gathers[j][3]()
    for c in z_copy:
        c.wait_send()
    for key in swaps:
        swaps[key][0].wait_send()
    for key in rings:
        for c in rings[key][0]:
            c.wait_send()
    ws[0][5]()
    ws[1][2]()
    ws[0][6]()
    ws[1][3]()
    ws[1][4]()
    ws[1][5]()
    ws[1][6]()


def slot_table(coords, count):
    index = jnp.arange(CAP, dtype=jnp.int32)
    live = index < count
    rows, cols = coords[:, 0], coords[:, 1]
    key = jnp.where(live, cols * 32 + rows, 4096 + index)
    rank = jnp.sum((key[None, :] < key[:, None]).astype(jnp.int32), axis=1)
    hit = rank[None, :] == index[:, None]
    pick = lambda v: jnp.sum(jnp.where(hit, v[None, :], 0), axis=1)
    first = jnp.ones((CAP,), jnp.int32)
    order, srow, scol = pick(index), pick(rows), pick(cols)
    first = jnp.concatenate([first[:1], (scol[1:] != scol[:-1]).astype(jnp.int32)])
    lanes = jnp.arange(COLS, dtype=jnp.int32)[:, None]
    upto = jnp.sum((live & (cols <= lanes)).astype(jnp.int32), axis=1)
    has = jnp.any(live & (cols == lanes), axis=1)
    end = jnp.where(has, upto - 1, -1)
    return order, srow, first, end


def body(grad_out, features, weight, degrees, block_coords, block_values, block_counts):
    table = slot_table(block_coords[0, 0], block_counts[0, 0])
    vm = lambda *s: pltpu.VMEM(s, BF16)
    vf = lambda *s: pltpu.VMEM(s, F32)
    dma = lambda *s: pltpu.SemaphoreType.DMA(s)
    any_spec, vmem_spec = pl.BlockSpec(memory_space=pl.ANY), pl.BlockSpec(memory_space=pltpu.VMEM)
    return pl.pallas_call(
        fused,
        out_shape=(jax.ShapeDtypeStruct((384, 512), BF16), jax.ShapeDtypeStruct((512, 512), F32)),
        in_specs=[pl.BlockSpec(memory_space=pltpu.SMEM)] * 4 + [any_spec, vmem_spec, vmem_spec, vmem_spec, vmem_spec],
        out_specs=(vmem_spec, vmem_spec),
        scratch_shapes=[
            vm(CAP, EDGE, EDGE), vm(24, EDGE, EDGE), vm(24, EDGE, EDGE), vm(24, EDGE, EDGE), vm(24, EDGE, EDGE), vm(CAP, EDGE, EDGE), vm(PARTS, 2, COLS, HALF, EDGE),
            vm(PARTS, 2, 2, 12, HALF, EDGE), vm(PARTS, 2, 2, 24, HALF, EDGE), vm(PARTS, 2, 24, HALF, EDGE),
            vm(PARTS, 2, 2, 3, HALF, EDGE), vm(PARTS, 2, 2, 6, HALF, EDGE), vm(PARTS, 2, 2, PER, HALF, EDGE),
            vm(PARTS, 2, PER, HALF, EDGE), vm(384, 512), vf(384, 128), vm(2, 48, HALF, EDGE),
            vm(2, 16, 32, 128), vf(2, 16, 32, 128), vm(2, 16, 32, 128), vm(2, 16, 32, 128), vm(2, 16, 32, 128),
            vm(2, 8, 32, 128), vm(2, 16, 32, 128), vm(2, 16, 32, 128),
            pltpu.SemaphoreType.DMA, dma(2, 4), dma(2, 4), dma(PARTS, 8), dma(PARTS, 8), dma(PARTS, 2, 2, 6), dma(PARTS, 2, 2, 6),
            dma(PARTS), dma(PARTS), dma(2, 2), dma(2, 2),
            dma(2, 2), dma(2, 2), dma(2), dma(2),
        ],
        compiler_params=pltpu.CompilerParams(
            collective_id=0, has_side_effects=True, vmem_limit_bytes=60 * 1024 * 1024
        ),
    )(*table, block_values[0, 0], grad_out, degrees.reshape(PER, 128), features, weight)


def solution(mesh):
    in_specs = (
        P(("row", "col"), None),
        P(("row", "col"), None),
        P(),
        P(("row", "col")),
        P("row", "col", None, None),
        P("row", "col", None, None, None),
        P("row", "col"),
    )
    out_specs = (P(("row", "col"), None), P())
    return jax.shard_map(body, mesh=mesh, in_specs=in_specs, out_specs=out_specs, check_vma=False)
```

time: 152 us -> 139 us (0.914)
  Pallas kernels: 143 us -> 131 us
    pallas_call x1, Pallas kernels: 143 us -> 131 us  [body(): pl.pallas_call(fused, out_shape=(jax.ShapeDtypeStruct((384, 512), BF16),...]
where the time goes in v3:
time: 139 us
  Pallas kernels  131 us (94%)
  local copies, waits for them, and re-layouts  4.03 us (3%)
  other arithmetic  3.29 us (2%)
    pallas_call x1, Pallas kernels, body(): pl.pallas_call(fused, out_shape=(jax.ShapeDtypeStruct((384, 512), BF16),...  131 us
    unnamed x2, local copies, waits for them, and re-layouts  4.03 us

profile of v3, /device:TPU:1, one launch (start us, length us, event | category | flops | bytes accessed | tf_op | source)
XLA Modules:
  0.0 139.2 jit_solution(6668334844816725867)
XLA Ops:
  1.3 0.8 compare_select_fusion
  2.1 0.2 convert_reduce_fusion
  2.3 0.1 convert_reduce_fusion.1
  2.4 0.1 fusion.1
  2.5 0.6 add_select_fusion.1.last_of
  3.1 0.8 select_reduce_fusion
  3.9 0.1 slice_compare_fusion
  3.9 0.6 add_convert_fusion.opens
  4.6 130.6 %shard_map.86 = (bf16[384,512]{1,0:T(8,128)(2,1)}, f32[512,512]{1,0:T(8,128)}) custom-call(s32[160]{0:T(256)} %get-tuple-element.4.slot_of, s32[160]{0:T(256)} %get-tuple-element.3.row_of, s32[160]{0:T(256)} %add_convert_fusion.opens, s32[96]{0:T(128)} %add_select_fusion.1.last_of, bf16[160,128,128]{2,1,0:T(8,128)(2,1)} %bitcast.10, ...), custom_call_target="tpu_custom_call" | custom-call | tf_op jit(solution)/shard_map/pallas_call | solution.py:465
  135.2 1.8 %copy.12 = bf16[384,512]{1,0:T(8,128)(2,1)} copy(bf16[384,512]{1,0:T(8,128)(2,1)} %get-tuple-element.10) | data formatting | bytes 786432
  136.9 2.3 %copy.13 = f32[512,512]{1,0:T(8,128)} copy(f32[512,512]{1,0:T(8,128)} %get-tuple-element.11) | data formatting | bytes 2097152
  (2 shorter events, 0.0 us)

commit v4 on v3

--- a/solution.py
+++ b/solution.py
@@ -438,6 +438,11 @@
     ws[1][6]()
 
 
+def ship(features, weight, out_features, out_weight):
+    out_weight[...] = weight[...]
+    out_features[...] = features[...]
+
+
 def slot_table(coords, count):
     index = jnp.arange(CAP, dtype=jnp.int32)
     live = index < count
@@ -462,9 +467,10 @@
     vf = lambda *s: pltpu.VMEM(s, F32)
     dma = lambda *s: pltpu.SemaphoreType.DMA(s)
     any_spec, vmem_spec = pl.BlockSpec(memory_space=pl.ANY), pl.BlockSpec(memory_space=pltpu.VMEM)
-    return pl.pallas_call(
+    shapes = (jax.ShapeDtypeStruct((384, 512), BF16), jax.ShapeDtypeStruct((512, 512), F32))
+    results = pl.pallas_call(
         fused,
-        out_shape=(jax.ShapeDtypeStruct((384, 512), BF16), jax.ShapeDtypeStruct((512, 512), F32)),
+        out_shape=shapes,
         in_specs=[pl.BlockSpec(memory_space=pltpu.SMEM)] * 4 + [any_spec, vmem_spec, vmem_spec, vmem_spec, vmem_spec],
         out_specs=(vmem_spec, vmem_spec),
         scratch_shapes=[
@@ -482,6 +488,12 @@
             collective_id=0, has_side_effects=True, vmem_limit_bytes=60 * 1024 * 1024
         ),
     )(*table, block_values[0, 0], grad_out, degrees.reshape(PER, 128), features, weight)
+    return pl.pallas_call(
+        ship,
+        out_shape=shapes,
+        in_specs=[vmem_spec, vmem_spec],
+        out_specs=(vmem_spec, vmem_spec),
+    )(*results)
 
 
 def solution(mesh):

time: 139 us -> 138 us (level)
  local copies, waits for them, and re-layouts: 4.03 us -> 0 us
  Pallas kernels: 131 us -> 133 us
    unnamed x2 -> x0, local copies, waits for them, and re-layouts: 4.03 us -> none
    pallas_call x1 -> x2, Pallas kernels: 131 us -> 133 us  [the longest x1 131 us: body(): pl.pallas_call(fused, out_shape=shapes, in_specs=[pl.BlockSpec(memory_spa...]
where the time goes in v4:
time: 138 us
  Pallas kernels  133 us (96%)
  other arithmetic  3.29 us (2%)
    pallas_call x1, Pallas kernels, body(): pl.pallas_call(fused, out_shape=shapes, in_specs=[pl.BlockSpec(memory_spa...  131 us

profile of v4, /device:TPU:1, one launch (start us, length us, event | category | flops | bytes accessed | tf_op | source)
XLA Modules:
  0.0 137.7 jit_solution(8195887071598886375)
XLA Ops:
  1.3 0.8 compare_select_fusion
  2.1 0.2 convert_reduce_fusion
  2.3 0.1 convert_reduce_fusion.1
  2.4 0.1 fusion.1
  2.5 0.6 add_select_fusion.1.last_of
  3.1 0.8 select_reduce_fusion
  3.9 0.1 slice_compare_fusion
  3.9 0.6 add_convert_fusion.opens
  4.6 130.6 %shard_map.86 = (bf16[384,512]{1,0:T(8,128)(2,1)}, f32[512,512]{1,0:T(8,128)}) custom-call(s32[160]{0:T(256)} %get-tuple-element.8.slot_of, s32[160]{0:T(256)} %get-tuple-element.7.row_of, s32[160]{0:T(256)} %add_convert_fusion.opens, s32[96]{0:T(128)} %add_select_fusion.1.last_of, bf16[160,128,128]{2,1,0:T(8,128)(2,1)} %bitcast.10, ...), custom_call_target="tpu_custom_call" | custom-call | tf_op jit(solution)/shard_map/pallas_call | solution.py:471
  135.2 2.5 %shard_map.87 = (bf16[384,512]{1,0:T(8,128)(2,1)}, f32[512,512]{1,0:T(8,128)}) custom-call(bf16[384,512]{1,0:T(8,128)(2,1)} %get-tuple-element.4.features, f32[512,512]{1,0:T(8,128)} %get-tuple-element.5.weight), custom_call_target="tpu_custom_call" | custom-call | tf_op jit(solution)/shard_map/pallas_call | solution.py:491
  (2 shorter events, 0.0 us)
